TPU v7x, 32 devices: a whole 2x2x4 slice. The times are simulated.
32 devices in a mesh: aux: 4 (over z), ao: 8 (over y, x, core).
Axes of the slice: x: 2, y: 2, z: 4, core: 2. Of those that a mesh axis runs over, the one named last changes fastest.
Arguments:
- soc_ints: bfloat16 [512, 3, 16, 8192], P('aux', None, None, 'ao'), may hold values from -6 to 6
- cou_ints: bfloat16 [512, 16, 8192], P('aux', None, 'ao'), may hold values from -6 to 6
- coef_t: bfloat16 [16, 8192], P(None, 'ao'), may hold values from -0.0625 to 0.0625
- active_rdm: float32 [16, 16], replicated, may hold values from -3 to 3
- spin_dens: bfloat16 [80, 256], P('ao'), may hold values from -6 to 6
- pair_list: int32 [80, 2], replicated, may hold values from 0 to 23
- owner_map: int32 [80], P('ao'), may hold values from 0 to 79, each once
- state_count: int32 [24], replicated, may hold values from 8 to 16, as said below
Outputs:
- soc_elems: float32 [3, 80], P(None, 'ao')
Inputs may be any that keep to these rules, and one draw needn't show every extreme that they name: `state_count`: each state's count of live active orbitals; some state has all 16. `owner_map`: every pair appears in exactly one slot.
All inputs are finite; a program needn't handle non-finite values.
Results may differ from a plain program's by a relative error of at most 0.0003.
Values may be sent and summed in bfloat16 or wider, within the bound.
A program may use at most 64 MiB of HBM per device.

v0:
```python
import jax
import jax.numpy as jnp
from jax import lax
from jax.sharding import PartitionSpec as P


def mean_field(soc_rows, cou_rows, active_rdm, scale):
    count = soc_rows.shape[0]
    width = active_rdm.shape[0]
    high = lax.Precision.HIGHEST
    fitted = jnp.dot(cou_rows, active_rdm.reshape(-1), precision=high)
    direct = jnp.einsum("p,pxk->xk", fitted, soc_rows, precision=high)
    folded = jnp.einsum(
        "vw,pwu->pvu", active_rdm, cou_rows.reshape(count, width, width), precision=high
    )
    crossed = jnp.einsum(
        "pxtv,pvu->xtu", soc_rows.reshape(count, 3, width, width), folded, precision=high
    )
    return (direct - 1.5 * crossed.reshape(3, width * width)) * scale


def transform(soc_ints, cou_ints, coef_t, count):
    width = coef_t.shape[0]
    span = soc_ints.shape[-1]
    soc_mo = jnp.einsum(
        "rn,un->ru", soc_ints.reshape(-1, span), coef_t, preferred_element_type=jnp.float32
    )
    cou_mo = jnp.einsum(
        "rn,un->ru", cou_ints.reshape(-1, span), coef_t, preferred_element_type=jnp.float32
    )
    return jnp.concatenate(
        [soc_mo.reshape(count, 3 * width * width), cou_mo.reshape(count, width * width)], axis=1
    )


def contract(field, dens_rows, pair_ids, pair_list, state_count, width):
    cells = width * width
    bra_state = jnp.take(pair_list[:, 0], pair_ids, axis=0)
    ket_state = jnp.take(pair_list[:, 1], pair_ids, axis=0)
    states = jnp.arange(state_count.shape[0], dtype=jnp.int32)
    bra_count = jnp.sum(
        jnp.where(bra_state[:, None] == states[None, :], state_count[None, :], 0), axis=1
    )
    ket_count = jnp.sum(
        jnp.where(ket_state[:, None] == states[None, :], state_count[None, :], 0), axis=1
    )
    live = jnp.minimum(bra_count, ket_count)
    cell = jnp.arange(cells, dtype=jnp.int32)
    inside = (cell[None, :] // width < live[:, None]) & (cell[None, :] % width < live[:, None])
    dens = jnp.where(inside, dens_rows.astype(jnp.float32), jnp.float32(0.0))
    return jnp.dot(field, dens.T, precision=lax.Precision.HIGHEST) / width


def on_device(soc_ints, cou_ints, coef_t, active_rdm, spin_dens, pair_list, owner_map, state_count):
    width = coef_t.shape[0]
    cells = width * width
    slab_rows = soc_ints.shape[0]
    total_aux = slab_rows * lax.axis_size("aux")
    scale = 1.0 / (8.0 * jnp.sqrt(jnp.float32(total_aux)))
    partial_rows = transform(soc_ints, cou_ints, coef_t, slab_rows)
    summed = lax.psum(partial_rows, "ao")
    local_field = mean_field(
        summed[:, : 3 * cells].reshape(slab_rows, 3, cells),
        summed[:, 3 * cells :],
        active_rdm,
        scale,
    )
    field = lax.psum(local_field, "aux")
    every_dens = lax.all_gather(spin_dens, "ao", axis=0, tiled=True)
    picked = jnp.take(every_dens, owner_map, axis=0)
    result = contract(field, picked, owner_map, pair_list, state_count, width)
    return result


def solution(mesh):
    return jax.shard_map(
        on_device,
        mesh=mesh,
        in_specs=(
            P("aux", None, None, "ao"),
            P("aux", None, "ao"),
            P(None, "ao"),
            P(),
            P("ao", None),
            P(),
            P("ao"),
            P(),
        ),
        out_specs=P(None, "ao"),
        check_vma=False,
    )
```

profile of v0, /device:TPU:0, one launch (start us, length us, event | category | flops | bytes accessed | tf_op | source)
XLA Modules:
  0.0 102.0 jit_solution(11540045527871964877)
XLA Ops:
  6.5 0.0 copy-start
  6.5 0.0 all-reduce.2.cloned.1.call-start
  6.5 0.8 copy-done
  7.3 6.4 %fusion.24 = f32[6144,16]{1,0:T(8,128)S(1)} fusion(bf16[6144,1024]{1,0:T(8,128)(2,1)} %bitcast.39, bf16[16,1024]{1,0:T(8,128)(2,1)S(1)} %copy-done), kind=kOutput, calls=%fused_computation.49 | convolution fusion | flops 201326592 | bytes 13008896 | tf_op jit(solution)/shard_map/rn,un->ru/dot_general | solution.py:25
  13.7 2.1 %reshape.95 = f32[128,768]{1,0:T(8,128)} reshape(f32[6144,16]{1,0:T(8,128)S(1)} %fusion.24) | data formatting | bytes 786432 | tf_op jit(solution)/shard_map/reshape | solution.py:32
  15.8 0.0 copy-start.3
  15.8 0.0 copy-start.5
  15.8 3.5 %fusion.25 = f32[2048,16]{1,0:T(8,128)S(1)} fusion(bf16[2048,1024]{1,0:T(8,128)(2,1)} %bitcast.40, bf16[16,1024]{1,0:T(8,128)(2,1)S(1)} %copy-done), kind=kOutput, calls=%fused_computation.50 | convolution fusion | flops 67108864 | bytes 4358144 | tf_op jit(solution)/shard_map/rn,un->ru/dot_general | solution.py:28
  19.3 0.4 reshape.97
  19.7 0.0 copy-done.1
  19.7 0.9 pad_maximum_fusion
  20.6 0.0 all-reduce.2.cloned.1.call-update
  20.6 0.0 copy-done.6
  20.6 0.0 copy-done.4
  20.7 0.7 gather_fusion.1
  21.3 0.7 gather_fusion.2
  22.0 0.1 reshape.134
  22.1 10.7 %all-gather = bf16[8,10,256]{2,1,0:T(8,128)(2,1)S(1)} all-gather(bf16[1,10,256]{2,1,0:T(8,128)(2,1)S(1)} %bitcast.44), channel_id=1, replica_groups=mesh['aux'=4,'ao'=8] {'ao'}, dimensions={0}, use_global_device_ids=true | all-gather | bytes 46080 | tf_op jit(solution)/shard_map/all_gather | solution.py:69
  32.8 0.6 gather_fusion
  33.4 0.2 select_reduce_fusion
  33.6 44.4 %all-reduce.2.cloned.1.call-done = f32[128,1024]{1,0:T(8,128)} async-done(((f32[128,1024]{1,0:T(8,128)}), f32[128,1024]{1,0:T(8,128)}) %all-reduce.2.cloned.1.call-update) | async-done | bytes 524304 | tf_op jit(solution)/shard_map/psum | solution.py:61
  78.0 1.0 %slice.23 = f32[128,768]{1,0:T(8,128)S(1)} slice(f32[128,1024]{1,0:T(8,128)} %all-reduce.2.cloned.1.call-done), slice={[0:128], [0:768]} | slice | bytes 786432 | tf_op jit(solution)/shard_map/slice | solution.py:63
  79.1 0.2 copy.25
  79.2 0.9 slice.22
  80.1 0.1 copy.27
  80.2 0.3 convolution_bitcast_fusion
  80.5 0.5 fusion
  81.1 0.1 mul.17
  81.2 1.1 %convolution_bitcast_fusion.2 = f32[128,1,1]{0,1,2:T(1,128)S(1)} fusion(f32[256,1]{0,1:T(1,128)S(1)} %reshape.134, f32[128,1024]{1,0:T(8,128)} %all-reduce.2.cloned.1.call-done), kind=kOutput, calls=%fused_computation.7 | convolution fusion | flops 393216 | bytes 132608 | tf_op jit(solution)/shard_map/dot_general | solution.py:11
  82.2 0.4 fusion.26
  82.7 11.6 %psum.15 = f32[3,256]{1,0:T(4,128)S(1)} all-reduce(f32[3,256]{1,0:T(4,128)S(1)} %fusion.17), channel_id=1, replica_groups=mesh['aux'=4,'ao'=8] {'aux'}, use_global_device_ids=true, to_apply=%region_1.0 | all-reduce | flops 768 | bytes 6144 | tf_op jit(solution)/shard_map/psum | solution.py:68
  94.3 0.8 convolution_multiply_fusion
  (16 shorter events, 0.1 us)
Async XLA Ops:
  6.5 0.8 copy-start
  6.5 71.5 %all-reduce.2.cloned.1.call-start = ((), (), s32[]{:S(2)}) async-start(), calls=%async_computation | async-start | bytes 1048576 | tf_op jit(solution)/shard_map/psum | solution.py:61
  15.8 3.9 %copy-start.1 = (f32[128,768]{1,0:T(8,128)S(1)}, f32[128,768]{1,0:T(8,128)}, u32[]{:S(2)}) copy-start(f32[128,768]{1,0:T(8,128)} %reshape.95) | copy-start | bytes 1179652
  15.8 4.8 %copy-start.6 = (s32[10]{0:T(128)S(1)}, s32[10]{0:T(128)}, u32[]{:S(2)}) copy-start(s32[10]{0:T(128)} %param.16) | copy-start | bytes 124
  15.8 4.9 %copy-start.4 = (s32[80,2]{0,1:T(2,128)S(1)}, s32[80,2]{0,1:T(2,128)}, u32[]{:S(2)}) copy-start(s32[80,2]{0,1:T(2,128)} %param.15) | copy-start | bytes 1924
  15.8 6.2 %copy-start.2 = (f32[16,16]{1,0:T(8,128)S(1)}, f32[16,16]{1,0:T(8,128)}, u32[]{:S(2)}) copy-start(f32[16,16]{1,0:T(8,128)} %param.13) | copy-start | bytes 3076
  15.8 6.3 %copy-start.3 = (bf16[10,256]{1,0:T(8,128)(2,1)S(1)}, bf16[10,256]{1,0:T(8,128)(2,1)}, u32[]{:S(2)}) copy-start(bf16[10,256]{1,0:T(8,128)(2,1)} %param.14) | copy-start | bytes 15364
  15.8 17.6 %copy-start.5 = (s32[24]{0:T(128)S(1)}, s32[24]{0:T(128)}, u32[]{:S(2)}) copy-start(s32[24]{0:T(128)} %param.17) | copy-start | bytes 292
Sparse Core Ops, SparseCore 0:
  20.7 57.2 all-reduce.1
where the time goes:
time: 102 us
  waiting for transfers between devices  44.5 us (44%)
  blocking collectives  22.3 us (22%)
  between operations  13.6 us (13%)
  matrix products  13 us (13%)
  local copies, waits for them, and re-layouts  7.58 us (7%)
  other arithmetic  1.08 us (1%)
    psum x1, waiting for transfers between devices, on_device(): summed = lax.psum(partial_rows, 'ao')  44.4 us
    psum x1, blocking collectives, on_device(): field = lax.psum(local_field, 'aux')  11.6 us
    all_gather x1, blocking collectives, on_device(): every_dens = lax.all_gather(spin_dens, 'ao', axis=0, tiled=True)  10.7 us
    dot_general x1, matrix products, transform(): jnp.einsum('rn,un->ru', soc_ints.reshape(-1, span), coef_t, preferred_ele...  6.39 us
    dot_general x1, matrix products, transform(): jnp.einsum('rn,un->ru', cou_ints.reshape(-1, span), coef_t, preferred_ele...  3.46 us
    reshape x1, local copies, waits for them, and re-layouts, transform(): soc_mo.reshape(count, 3 * width * width)  2.09 us
  transfers between devices with their start and end apart: 1, of which 1 were waited for; matrix products, arithmetic and copies ran while one was open for 2% of the time, Pallas kernels for 0%

commit v1 on v0

v1 whole, which is shorter than its diff:
```python
import functools

import jax
import jax.numpy as jnp
from jax import lax
from jax.experimental import pallas as pl
from jax.experimental.pallas import tpu as pltpu
from jax.sharding import PartitionSpec as P

MESH = pl.DeviceIdType.MESH
HIGH = lax.Precision.HIGHEST
NN = (((1,), (0,)), ((), ()))
NT = (((1,), (1,)), ((), ()))


def iota(shape, dim):
    return lax.broadcasted_iota(jnp.int32, shape, dim)


def dot(a, b, dims):
    return lax.dot_general(a, b, dims, precision=HIGH, preferred_element_type=jnp.float32)


def kernel(
    n, m, chunks, k, scale,
    soc_ref, cou_ref, coef_ref, rdm_ref, dens_ref, pair_ref, owner_ref, count_ref,
    out_ref,
    soc_v, cou_v, send, recv, dens_out, dens_all, dmat, fit_w, fold_w,
    part_a, part_b,
    soc_sem, cou_sem, send_sem, recv_sem, dsend_sem, drecv_sem,
    asend_sem, arecv_sem, bsend_sem, brecv_sem,
):
    width = rdm_ref.shape[0]
    own = dens_ref.shape[0]
    cells = width * width
    states = count_ref.shape[1]
    pairs = pair_ref.shape[1]
    rows_p = n * 16
    me = lax.axis_index("ao")
    z = lax.axis_index("aux")

    def peer(d):
        return lax.rem(me + 1 + d, n)

    def fetch(c, d):
        at = (c * n + peer(d)) * k
        return (
            pltpu.make_async_copy(soc_ref.at[pl.ds(at, k)], soc_v.at[pl.ds(at, k)], soc_sem.at[c, d]),
            pltpu.make_async_copy(cou_ref.at[pl.ds(at, k)], cou_v.at[pl.ds(at, k)], cou_sem.at[c, d]),
        )

    def start_fetch(i, carry):
        for copy in fetch(i // n, lax.rem(i, n)):
            copy.start()
        return carry

    lax.fori_loop(0, n, start_fetch, 0)

    barrier = pltpu.get_barrier_semaphore()
    for d in range(n - 1):
        pl.semaphore_signal(barrier, inc=1, device_id=(z, peer(d)), device_id_type=MESH)
    for d in range(m - 1):
        pl.semaphore_signal(
            barrier, inc=1, device_id=(lax.rem(z + 1 + d, m), me), device_id_type=MESH
        )

    lax.fori_loop(n, chunks * n, start_fetch, 0)

    dens = dens_ref[...].astype(jnp.float32)
    if own < 16:
        dens = jnp.concatenate([dens, jnp.zeros((16 - own, cells), jnp.float32)], axis=0)
    dens_out[...] = dens.astype(jnp.bfloat16)
    dens_all[me] = dens.astype(jnp.bfloat16)

    pl.semaphore_wait(barrier, n + m - 2)

    def dens_copy(d):
        return pltpu.make_async_remote_copy(
            src_ref=dens_out, dst_ref=dens_all.at[me], send_sem=dsend_sem, recv_sem=drecv_sem,
            device_id=(z, peer(d)), device_id_type=MESH,
        )

    def block_copy(c, d):
        j = peer(d)
        return pltpu.make_async_remote_copy(
            src_ref=send.at[c, j], dst_ref=recv.at[c, me],
            send_sem=send_sem.at[c], recv_sem=recv_sem.at[c],
            device_id=(z, j), device_id_type=MESH,
        )

    def transform(c, d):
        for copy in fetch(c, d):
            copy.wait()
        at = (c * n + peer(d)) * k
        span = soc_v.shape[-1]
        rows = jnp.concatenate(
            [
                soc_v[pl.ds(at, k)].reshape(3 * width * k, span),
                cou_v[pl.ds(at, k)].reshape(width * k, span),
            ],
            axis=0,
        )
        return lax.dot_general(coef_ref[...], rows, NT, preferred_element_type=jnp.float32)

    for d in range(n - 1):
        dens_copy(d).start()

    lanes = width * k
    rdm = rdm_ref[...]
    spread = (lax.rem(iota((width, lanes), 1), width) == iota((width, lanes), 0)).astype(jnp.float32)
    tiled = jnp.concatenate([rdm] * k, axis=0)
    eye = (iota((width, width), 0) == iota((width, width), 1)).astype(jnp.float32)
    fit_w[...] = dot(eye, tiled, NT)
    wide = dot(rdm, spread, NN)
    wide = jnp.concatenate([wide] * k, axis=0)
    same = iota((lanes, lanes), 0) // width == iota((lanes, lanes), 1) // width
    fold_w[...] = jnp.where(same, -1.5 * wide, 0.0)

    def chunk(c, carry):
        def one(d, carry):
            send[c, peer(d)] = transform(c, d)
            block_copy(c, d).start()
            return carry

        lax.fori_loop(0, n - 1, one, 0)
        recv[c, me] = transform(c, n - 1)
        return carry

    lax.fori_loop(0, chunks, chunk, 0)

    pltpu.make_async_copy(
        dens_all.at[pl.ds(0, n - 1)], dens_all.at[pl.ds(0, n - 1)], drecv_sem
    ).wait()
    bra = iota((states, pairs), 0) == pair_ref[0:1, :]
    ket = iota((states, pairs), 0) == pair_ref[1:2, :]
    counts = jnp.broadcast_to(count_ref[...].astype(jnp.float32), (8, states))
    bra_count = dot(counts, bra.astype(jnp.float32), NN)
    ket_count = dot(counts, ket.astype(jnp.float32), NN)
    live_row = jnp.minimum(bra_count, ket_count)[0:1, :]
    row = iota((rows_p, pairs), 0)
    place = (lax.rem(row, 16) < own) & (row // 16 * own + lax.rem(row, 16) == iota((rows_p, pairs), 1))
    live = jnp.sum(jnp.where(place, live_row, 0.0), axis=1, keepdims=True).astype(jnp.int32)
    cell = iota((rows_p, cells), 1)
    inside = (cell // width < live) & (lax.rem(cell, width) < live)
    dmat[...] = jnp.where(inside, dens_all[...].astype(jnp.float32).reshape(rows_p, cells), 0.0)

    total = []
    for c in range(chunks):
        block = recv.at[c, pl.ds(0, n - 1)]
        pltpu.make_async_copy(block, block, recv_sem.at[c]).wait()
        summed = recv[c, 0]
        for s in range(1, n):
            summed = summed + recv[c, s]
        total.append(summed)

    cou_t = jnp.concatenate([t[:, 3 * lanes:] for t in total], axis=0)
    fit_in = cou_t * jnp.concatenate([fit_w[...]] * chunks, axis=0)
    fit_in = jnp.broadcast_to(
        jnp.sum(fit_in.reshape(chunks, width, lanes), axis=1, keepdims=True), (chunks, width, lanes)
    ).reshape(chunks * width, lanes)
    fitted = dot(fit_in, same.astype(jnp.float32), NN)
    down = iota((chunks * width, lanes), 0)
    across = iota((chunks * width, lanes), 1)
    diagonal = lax.rem(down, width) == lax.rem(across, width)
    mixed = dot(cou_t, fold_w[...], NT) + jnp.where(diagonal, fitted, 0.0)
    field = None
    for c in range(chunks):
        stacked = jnp.concatenate(
            [total[c][:, 3 * width * p: 3 * width * (p + 1)] for p in range(k)], axis=0
        )
        term = dot(mixed[c * width:(c + 1) * width], stacked, NN)
        field = term if field is None else field + term
    field = field * scale

    deep = 3 * width
    keep = iota((cells, deep), 0) // width == lax.rem(iota((cells, deep), 1), width)
    laid = jnp.where(keep, jnp.concatenate([field] * width, axis=0), 0.0)
    pick = (iota((8, deep), 1) // width == iota((8, deep), 0)).astype(jnp.float32)
    flat = dot(pick, laid, NT)
    value = dot(flat, dmat[...], NT)

    part_a[me] = value

    def a_copy(d):
        return pltpu.make_async_remote_copy(
            src_ref=part_a.at[me], dst_ref=part_a.at[me], send_sem=asend_sem, recv_sem=arecv_sem,
            device_id=(z, peer(d)), device_id_type=MESH,
        )

    for d in range(n - 1):
        a_copy(d).start()
    block = part_a.at[pl.ds(0, n - 1)]
    pltpu.make_async_copy(block, block, arecv_sem).wait()
    value = part_a[0]
    for s in range(1, n):
        value = value + part_a[s]

    part_b[z] = value

    def b_copy(d):
        return pltpu.make_async_remote_copy(
            src_ref=part_b.at[z], dst_ref=part_b.at[z], send_sem=bsend_sem, recv_sem=brecv_sem,
            device_id=(lax.rem(z + 1 + d, m), me), device_id_type=MESH,
        )

    for d in range(m - 1):
        b_copy(d).start()
    block = part_b.at[pl.ds(0, m - 1)]
    pltpu.make_async_copy(block, block, brecv_sem).wait()
    value = part_b[0]
    for s in range(1, m):
        value = value + part_b[s]

    slots = owner_ref.shape[1]
    row = iota((rows_p, slots), 0)
    chosen = (lax.rem(row, 16) < own) & (row // 16 * own + lax.rem(row, 16) == owner_ref[...])
    out_ref[...] = dot(value, chosen.astype(jnp.float32), NN)[0:3, :]

    pltpu.make_async_copy(
        dens_all.at[pl.ds(0, n - 1)], dens_all.at[pl.ds(0, n - 1)], dsend_sem
    ).wait()
    for c in range(chunks):
        block = send.at[c, pl.ds(0, n - 1)]
        pltpu.make_async_copy(block, block, send_sem.at[c]).wait()
    block = part_a.at[pl.ds(0, n - 1)]
    pltpu.make_async_copy(block, block, asend_sem).wait()
    block = part_b.at[pl.ds(0, m - 1)]
    pltpu.make_async_copy(block, block, bsend_sem).wait()


def on_device(n, m, soc_ints, cou_ints, coef_t, active_rdm, spin_dens, pair_list, owner_map, state_count):
    slab, parts, width, span = soc_ints.shape
    k = max(1, slab // (n * 4))
    chunks = slab // (n * k)
    block = (parts + 1) * width * k
    own, cells = spin_dens.shape
    rows_p = n * 16
    scale = 1.0 / (8.0 * float(slab * m) ** 0.5 * width)
    vmem = pl.BlockSpec(memory_space=pltpu.VMEM)
    hbm = pl.BlockSpec(memory_space=pl.ANY)
    dma = pltpu.SemaphoreType.DMA
    return pl.pallas_call(
        functools.partial(kernel, n, m, chunks, k, scale),
        out_shape=jax.ShapeDtypeStruct((parts, owner_map.shape[0]), jnp.float32),
        in_specs=[hbm, hbm] + [vmem] * 6,
        out_specs=vmem,
        scratch_shapes=[
            pltpu.VMEM((slab, parts * width, span), jnp.bfloat16),
            pltpu.VMEM((slab, width, span), jnp.bfloat16),
            pltpu.VMEM((chunks, n, width, block), jnp.float32),
            pltpu.VMEM((chunks, n, width, block), jnp.float32),
            pltpu.VMEM((16, cells), jnp.bfloat16),
            pltpu.VMEM((n, 16, cells), jnp.bfloat16),
            pltpu.VMEM((rows_p, cells), jnp.float32),
            pltpu.VMEM((width, width * k), jnp.float32),
            pltpu.VMEM((width * k, width * k), jnp.float32),
            pltpu.VMEM((n, 8, rows_p), jnp.float32),
            pltpu.VMEM((m, 8, rows_p), jnp.float32),
            dma((chunks, n)), dma((chunks, n)), dma((chunks,)), dma((chunks,)),
            dma, dma, dma, dma, dma, dma,
        ],
        compiler_params=pltpu.CompilerParams(
            collective_id=0, has_side_effects=True, vmem_limit_bytes=60 * 1024 * 1024
        ),
        cost_estimate=pl.CostEstimate(
            flops=2 * slab * 4 * width * width * span, bytes_accessed=slab * 4 * width * span * 2,
            transcendentals=0,
        ),
    )(
        soc_ints.reshape(slab, parts * width, span), cou_ints, coef_t, active_rdm, spin_dens,
        pair_list.T, owner_map.reshape(1, -1), state_count.reshape(1, -1),
    )


def solution(mesh):
    return jax.shard_map(
        functools.partial(on_device, mesh.shape["ao"], mesh.shape["aux"]),
        mesh=mesh,
        in_specs=(
            P("aux", None, None, "ao"),
            P("aux", None, "ao"),
            P(None, "ao"),
            P(),
            P("ao", None),
            P(),
            P("ao"),
            P(),
        ),
        out_specs=P(None, "ao"),
        check_vma=False,
    )
```

time: 102 us -> 28.2 us (0.28)
  waiting for transfers between devices: 44.5 us -> 0 us
  Pallas kernels: 0 us -> 26.8 us
  blocking collectives: 22.3 us -> 0 us
  between operations: 13.6 us -> 0.01 us
  matrix products: 13 us -> 0 us
  local copies, waits for them, and re-layouts: 7.58 us -> 1.26 us
  other arithmetic: 1.08 us -> 0 us
    psum x1 -> x0, waiting for transfers between devices: 44.4 us -> none  [on_device(): summed = lax.psum(partial_rows, 'ao')]
    pallas_call x0 -> x1, Pallas kernels: none -> 26.8 us  [on_device(): pl.pallas_call(functools.partial(kernel, n, m, chunks, k, scale), out_sha...]
    dot_general x7 -> x0, matrix products: 13 us -> none  [the longest x1 6.39 us: transform(): jnp.einsum('rn,un->ru', soc_ints.reshape(-1, span), coef_t, preferred_ele...]
    psum x1 -> x0, blocking collectives: 11.6 us -> none  [on_device(): field = lax.psum(local_field, 'aux')]
    all_gather x1 -> x0, blocking collectives: 10.7 us -> none  [on_device(): every_dens = lax.all_gather(spin_dens, 'ao', axis=0, tiled=True)]
    reshape x3 -> x0, local copies, waits for them, and re-layouts: 2.61 us -> none  [the longest x1 2.09 us: transform(): soc_mo.reshape(count, 3 * width * width)]
    slice x4 -> x0, local copies, waits for them, and re-layouts: 2.18 us -> none  [the longest x2 1.18 us: on_device(): summed[:, :3 * cells].reshape(slab_rows, 3, cells)]
    gather x3 -> x0, local copies, waits for them, and re-layouts: 1.9 us -> none  [the longest x1 0.66 us: contract(): ket_state = jnp.take(pair_list[:, 1], pair_ids, axis=0)]
  transfers between devices with their start and end apart: 1 -> 0, of which waited for: 1 -> 0; matrix products, arithmetic and copies ran while one was open for 2% -> 0% of each run, Pallas kernels for 0% -> 0%
where the time goes in v1:
time: 28.2 us; the launch traced here: 28 us
  Pallas kernels  26.8 us (95%)
  local copies, waits for them, and re-layouts  1.26 us (4%)
    pallas_call x1, Pallas kernels, on_device(): pl.pallas_call(functools.partial(kernel, n, m, chunks, k, scale), out_sha...  26.8 us
    unnamed x1, local copies, waits for them, and re-layouts  1.26 us

profile of v1, /device:TPU:0, one launch (start us, length us, event | category | flops | bytes accessed | tf_op | source)
XLA Modules:
  0.0 28.0 jit_solution(14412751896448391663)
XLA Ops:
  0.0 26.8 %shard_map.82 = f32[3,10]{1,0:T(4,128)} custom-call(bf16[128,48,1024]{2,1,0:T(8,128)(2,1)} %bitcast.4, bf16[128,16,1024]{2,1,0:T(8,128)(2,1)} %cou_ref.1, bf16[16,1024]{1,0:T(8,128)(2,1)} %coef_ref.1, f32[16,16]{1,0:T(8,128)} %rdm_ref.1, bf16[10,256]{1,0:T(8,128)(2,1)} %dens_ref.1, s32[2,80]{1,0:T(2,128)} %bitcast.5, s32[1,10]{1,0:T(1,128)} %bitcast.6, ...), custom_call_target="tpu_custom_call" | custom-call | flops 268435456 | bytes 16777216 | tf_op jit(solution)/shard_map/pallas_call | solution.py:242
  26.8 1.3 %copy.10 = f32[3,10]{1,0:T(4,128)} copy(f32[3,10]{1,0:T(4,128)} %shard_map.82) | data formatting | bytes 240

commit v2 on v1

--- a/solution.py
+++ b/solution.py
@@ -21,10 +21,25 @@
     return lax.dot_general(a, b, dims, precision=HIGH, preferred_element_type=jnp.float32)
 
 
+def parts_of(x):
+    hi = x.astype(jnp.bfloat16)
+    rest = x - hi.astype(jnp.float32)
+    mid = rest.astype(jnp.bfloat16)
+    return hi, mid, (rest - mid.astype(jnp.float32)).astype(jnp.bfloat16)
+
+
+def exact_dot(x, table, dims):
+    rows = x.shape[0]
+    stack = jnp.concatenate([p.astype(jnp.float32) for p in parts_of(x)], axis=0).astype(jnp.bfloat16)
+    out = lax.dot_general(stack, table.astype(jnp.bfloat16), dims, preferred_element_type=jnp.float32)
+    return out[:rows] + out[rows:2 * rows] + out[2 * rows:3 * rows]
+
+
 def kernel(
-    n, m, chunks, k, scale,
-    soc_ref, cou_ref, coef_ref, rdm_ref, dens_ref, pair_ref, owner_ref, count_ref,
+    n, m, chunks, k, group, scale,
+    soc_ref, cou_ref, coef_hbm, rdm_hbm, dens_hbm, pair_hbm, owner_hbm, count_hbm,
     out_ref,
+    coef_ref, rdm_ref, dens_ref, pair_ref, owner_ref, count_ref, small_sem,
     soc_v, cou_v, send, recv, dens_out, dens_all, dmat, fit_w, fold_w,
     part_a, part_b,
     soc_sem, cou_sem, send_sem, recv_sem, dsend_sem, drecv_sem,
@@ -40,7 +55,8 @@
     z = lax.axis_index("aux")
 
     def peer(d):
-        return lax.rem(me + 1 + d, n)
+        chip = lax.rem(me // 2 + 1 + d // 2, n // 2)
+        return chip * 2 + lax.rem(me + 1 + d, 2)
 
     def fetch(c, d):
         at = (c * n + peer(d)) * k
@@ -54,7 +70,16 @@
             copy.start()
         return carry
 
-    lax.fori_loop(0, n, start_fetch, 0)
+    lax.fori_loop(0, group, start_fetch, 0)
+    small = [
+        pltpu.make_async_copy(a, b, small_sem.at[i])
+        for i, (a, b) in enumerate([
+            (coef_hbm, coef_ref), (rdm_hbm, rdm_ref), (dens_hbm, dens_ref),
+            (pair_hbm, pair_ref), (owner_hbm, owner_ref), (count_hbm, count_ref),
+        ])
+    ]
+    for copy in small:
+        copy.start()
 
     barrier = pltpu.get_barrier_semaphore()
     for d in range(n - 1):
@@ -64,7 +89,9 @@
             barrier, inc=1, device_id=(lax.rem(z + 1 + d, m), me), device_id_type=MESH
         )
 
-    lax.fori_loop(n, chunks * n, start_fetch, 0)
+    lax.fori_loop(group, chunks * n, start_fetch, 0)
+    for copy in small:
+        copy.wait()
 
     dens = dens_ref[...].astype(jnp.float32)
     if own < 16:
@@ -88,19 +115,22 @@
             device_id=(z, j), device_id_type=MESH,
         )
 
-    def transform(c, d):
-        for copy in fetch(c, d):
-            copy.wait()
-        at = (c * n + peer(d)) * k
-        span = soc_v.shape[-1]
-        rows = jnp.concatenate(
-            [
-                soc_v[pl.ds(at, k)].reshape(3 * width * k, span),
-                cou_v[pl.ds(at, k)].reshape(width * k, span),
-            ],
-            axis=0,
-        )
-        return lax.dot_general(coef_ref[...], rows, NT, preferred_element_type=jnp.float32)
+    span = soc_v.shape[-1]
+    block_rows = 4 * width * k
+
+    def transform(c, first):
+        for i in range(group):
+            for copy in fetch(c, first + i):
+                copy.wait()
+        rows = []
+        for i in range(group):
+            at = (c * n + peer(first + i)) * k
+            rows.append(soc_v[pl.ds(at, k)].reshape(3 * width * k, span))
+            rows.append(cou_v[pl.ds(at, k)].reshape(width * k, span))
+        out = lax.dot_general(
+            coef_ref[...], jnp.concatenate(rows, axis=0), NT, preferred_element_type=jnp.float32
+        )
+        return [out[:, i * block_rows:(i + 1) * block_rows] for i in range(group)]
 
     for d in range(n - 1):
         dens_copy(d).start()
@@ -117,13 +147,20 @@
     fold_w[...] = jnp.where(same, -1.5 * wide, 0.0)
 
     def chunk(c, carry):
-        def one(d, carry):
-            send[c, peer(d)] = transform(c, d)
-            block_copy(c, d).start()
+        def one(g, carry):
+            for i, block in enumerate(transform(c, g * group)):
+                send[c, peer(g * group + i)] = block
+                block_copy(c, g * group + i).start()
             return carry
 
-        lax.fori_loop(0, n - 1, one, 0)
-        recv[c, me] = transform(c, n - 1)
+        lax.fori_loop(0, n // group - 1, one, 0)
+        last = n - group
+        for i, block in enumerate(transform(c, last)):
+            if i < group - 1:
+                send[c, peer(last + i)] = block
+                block_copy(c, last + i).start()
+            else:
+                recv[c, me] = block
         return carry
 
     lax.fori_loop(0, chunks, chunk, 0)
@@ -133,9 +170,13 @@
     ).wait()
     bra = iota((states, pairs), 0) == pair_ref[0:1, :]
     ket = iota((states, pairs), 0) == pair_ref[1:2, :]
-    counts = jnp.broadcast_to(count_ref[...].astype(jnp.float32), (8, states))
-    bra_count = dot(counts, bra.astype(jnp.float32), NN)
-    ket_count = dot(counts, ket.astype(jnp.float32), NN)
+    counts = jnp.broadcast_to(count_ref[...].astype(jnp.float32), (8, states)).astype(jnp.bfloat16)
+    bra_count = lax.dot_general(
+        counts, bra.astype(jnp.float32).astype(jnp.bfloat16), NN, preferred_element_type=jnp.float32
+    )
+    ket_count = lax.dot_general(
+        counts, ket.astype(jnp.float32).astype(jnp.bfloat16), NN, preferred_element_type=jnp.float32
+    )
     live_row = jnp.minimum(bra_count, ket_count)[0:1, :]
     row = iota((rows_p, pairs), 0)
     place = (lax.rem(row, 16) < own) & (row // 16 * own + lax.rem(row, 16) == iota((rows_p, pairs), 1))
@@ -158,26 +199,27 @@
     fit_in = jnp.broadcast_to(
         jnp.sum(fit_in.reshape(chunks, width, lanes), axis=1, keepdims=True), (chunks, width, lanes)
     ).reshape(chunks * width, lanes)
-    fitted = dot(fit_in, same.astype(jnp.float32), NN)
+    fitted = exact_dot(fit_in, same.astype(jnp.float32), NN)
     down = iota((chunks * width, lanes), 0)
     across = iota((chunks * width, lanes), 1)
     diagonal = lax.rem(down, width) == lax.rem(across, width)
     mixed = dot(cou_t, fold_w[...], NT) + jnp.where(diagonal, fitted, 0.0)
-    field = None
-    for c in range(chunks):
-        stacked = jnp.concatenate(
-            [total[c][:, 3 * width * p: 3 * width * (p + 1)] for p in range(k)], axis=0
-        )
-        term = dot(mixed[c * width:(c + 1) * width], stacked, NN)
-        field = term if field is None else field + term
-    field = field * scale
+    stacked = jnp.concatenate(
+        [t[:, 3 * width * p: 3 * width * (p + 1)] for t in total for p in range(k)], axis=0
+    )
+    mixed = jnp.concatenate([mixed[c * width:(c + 1) * width] for c in range(chunks)], axis=1)
+    field = dot(mixed, stacked, NN) * scale
 
     deep = 3 * width
-    keep = iota((cells, deep), 0) // width == lax.rem(iota((cells, deep), 1), width)
-    laid = jnp.where(keep, jnp.concatenate([field] * width, axis=0), 0.0)
-    pick = (iota((8, deep), 1) // width == iota((8, deep), 0)).astype(jnp.float32)
-    flat = dot(pick, laid, NT)
-    value = dot(flat, dmat[...], NT)
+    laid = jnp.concatenate([p.astype(jnp.float32) for p in parts_of(field)], axis=1)
+    laid = jnp.concatenate([laid] * width, axis=0)
+    keep = iota((cells, 3 * deep), 0) // width == lax.rem(iota((cells, 3 * deep), 1), width)
+    laid = jnp.where(keep, laid, 0.0).astype(jnp.bfloat16)
+    pick = lax.rem(iota((8, 3 * deep), 1), deep) // width == iota((8, 3 * deep), 0)
+    flat = lax.dot_general(
+        pick.astype(jnp.float32).astype(jnp.bfloat16), laid, NT, preferred_element_type=jnp.float32
+    )
+    value = exact_dot(flat, dmat[...], NT)
 
     part_a[me] = value
 
@@ -214,7 +256,7 @@
     slots = owner_ref.shape[1]
     row = iota((rows_p, slots), 0)
     chosen = (lax.rem(row, 16) < own) & (row // 16 * own + lax.rem(row, 16) == owner_ref[...])
-    out_ref[...] = dot(value, chosen.astype(jnp.float32), NN)[0:3, :]
+    out_ref[...] = exact_dot(value, chosen.astype(jnp.float32), NN)[0:3, :]
 
     pltpu.make_async_copy(
         dens_all.at[pl.ds(0, n - 1)], dens_all.at[pl.ds(0, n - 1)], dsend_sem
@@ -240,11 +282,18 @@
     hbm = pl.BlockSpec(memory_space=pl.ANY)
     dma = pltpu.SemaphoreType.DMA
     return pl.pallas_call(
-        functools.partial(kernel, n, m, chunks, k, scale),
+        functools.partial(kernel, n, m, chunks, k, 4, scale),
         out_shape=jax.ShapeDtypeStruct((parts, owner_map.shape[0]), jnp.float32),
-        in_specs=[hbm, hbm] + [vmem] * 6,
+        in_specs=[hbm] * 8,
         out_specs=vmem,
         scratch_shapes=[
+            pltpu.VMEM((width, span), jnp.bfloat16),
+            pltpu.VMEM((width, width), jnp.float32),
+            pltpu.VMEM((own, cells), jnp.bfloat16),
+            pltpu.VMEM((2, pair_list.shape[0]), jnp.int32),
+            pltpu.VMEM((1, own), jnp.int32),
+            pltpu.VMEM((1, state_count.shape[0]), jnp.int32),
+            dma((6,)),
             pltpu.VMEM((slab, parts * width, span), jnp.bfloat16),
             pltpu.VMEM((slab, width, span), jnp.bfloat16),
             pltpu.VMEM((chunks, n, width, block), jnp.float32),

time: 28.2 us -> 25.1 us (0.89)
  Pallas kernels: 26.8 us -> 23.6 us
    pallas_call x1, Pallas kernels: 26.8 us -> 23.6 us  [on_device(): pl.pallas_call(functools.partial(kernel, n, m, chunks, k, 4, scale), out_...]
where the time goes in v2:
time: 25.1 us; the launch traced here: 24.9 us
  Pallas kernels  23.6 us (94%)
  local copies, waits for them, and re-layouts  1.26 us (5%)
    pallas_call x1, Pallas kernels, on_device(): pl.pallas_call(functools.partial(kernel, n, m, chunks, k, 4, scale), out_...  23.6 us
    unnamed x1, local copies, waits for them, and re-layouts  1.26 us

profile of v2, /device:TPU:0, one launch (start us, length us, event | category | flops | bytes accessed | tf_op | source)
XLA Modules:
  0.0 24.9 jit_solution(6170171718384430653)
XLA Ops:
  0.0 23.6 %shard_map.82 = f32[3,10]{1,0:T(4,128)} custom-call(bf16[128,48,1024]{2,1,0:T(8,128)(2,1)} %bitcast.4, bf16[128,16,1024]{2,1,0:T(8,128)(2,1)} %cou_ref.1, bf16[16,1024]{1,0:T(8,128)(2,1)} %coef_hbm.1, f32[16,16]{1,0:T(8,128)} %rdm_hbm.1, bf16[10,256]{1,0:T(8,128)(2,1)} %dens_hbm.1, s32[2,80]{1,0:T(2,128)} %bitcast.5, s32[1,10]{1,0:T(1,128)} %bitcast.6, ...), custom_call_target="tpu_custom_call" | custom-call | flops 268435456 | bytes 16777216 | tf_op jit(solution)/shard_map/pallas_call | solution.py:284
  23.6 1.3 %copy.10 = f32[3,10]{1,0:T(4,128)} copy(f32[3,10]{1,0:T(4,128)} %shard_map.82) | data formatting | bytes 240

commit v3 on v2

--- a/solution.py
+++ b/solution.py
@@ -128,8 +128,8 @@
             rows.append(soc_v[pl.ds(at, k)].reshape(3 * width * k, span))
             rows.append(cou_v[pl.ds(at, k)].reshape(width * k, span))
         out = lax.dot_general(
-            coef_ref[...], jnp.concatenate(rows, axis=0), NT, preferred_element_type=jnp.float32
-        )
+            jnp.concatenate(rows, axis=0), coef_ref[...], NT, preferred_element_type=jnp.float32
+        ).T
         return [out[:, i * block_rows:(i + 1) * block_rows] for i in range(group)]
 
     for d in range(n - 1):

time: 25.1 us -> 29.5 us (1.18)
  Pallas kernels: 23.6 us -> 28.1 us
    pallas_call x1, Pallas kernels: 23.6 us -> 28.1 us  [on_device(): pl.pallas_call(functools.partial(kernel, n, m, chunks, k, 4, scale), out_...]
where the time goes in v3:
time: 29.5 us; the launch traced here: 29.4 us
  Pallas kernels  28.1 us (95%)
  local copies, waits for them, and re-layouts  1.26 us (4%)
    pallas_call x1, Pallas kernels, on_device(): pl.pallas_call(functools.partial(kernel, n, m, chunks, k, 4, scale), out_...  28.1 us
    unnamed x1, local copies, waits for them, and re-layouts  1.26 us

profile of v3, /device:TPU:0, one launch (start us, length us, event | category | flops | bytes accessed | tf_op | source)
XLA Modules:
  0.0 29.4 jit_solution(15823819727068949555)
XLA Ops:
  0.0 28.1 %shard_map.82 = f32[3,10]{1,0:T(4,128)} custom-call(bf16[128,48,1024]{2,1,0:T(8,128)(2,1)} %bitcast.4, bf16[128,16,1024]{2,1,0:T(8,128)(2,1)} %cou_ref.1, bf16[16,1024]{1,0:T(8,128)(2,1)} %coef_hbm.1, f32[16,16]{1,0:T(8,128)} %rdm_hbm.1, bf16[10,256]{1,0:T(8,128)(2,1)} %dens_hbm.1, s32[2,80]{1,0:T(2,128)} %bitcast.5, s32[1,10]{1,0:T(1,128)} %bitcast.6, ...), custom_call_target="tpu_custom_call" | custom-call | flops 268435456 | bytes 16777216 | tf_op jit(solution)/shard_map/pallas_call | solution.py:284
  28.1 1.3 %copy.10 = f32[3,10]{1,0:T(4,128)} copy(f32[3,10]{1,0:T(4,128)} %shard_map.82) | data formatting | bytes 240

commit v4 on v2

--- a/solution.py
+++ b/solution.py
@@ -40,9 +40,9 @@
     soc_ref, cou_ref, coef_hbm, rdm_hbm, dens_hbm, pair_hbm, owner_hbm, count_hbm,
     out_ref,
     coef_ref, rdm_ref, dens_ref, pair_ref, owner_ref, count_ref, small_sem,
-    soc_v, cou_v, send, recv, dens_out, dens_all, dmat, fit_w, fold_w,
+    soc_v, cou_v, sib_send, sib_recv, mine, recv, dens_out, dens_all, dmat, fit_w, fold_w,
     part_a, part_b,
-    soc_sem, cou_sem, send_sem, recv_sem, dsend_sem, drecv_sem,
+    soc_sem, cou_sem, sib_ssem, sib_rsem, send_sem, recv_sem, dsend_sem, drecv_sem,
     asend_sem, arecv_sem, bsend_sem, brecv_sem,
 ):
     width = rdm_ref.shape[0]
@@ -53,10 +53,14 @@
     rows_p = n * 16
     me = lax.axis_index("ao")
     z = lax.axis_index("aux")
+    q = n // 2
+    my_chip = me // 2
+    core = lax.rem(me, 2)
+    sibling = my_chip * 2 + 1 - core
 
     def peer(d):
-        chip = lax.rem(me // 2 + 1 + d // 2, n // 2)
-        return chip * 2 + lax.rem(me + 1 + d, 2)
+        chip = lax.rem(my_chip + 1 + lax.rem(d, q), q)
+        return chip * 2 + lax.rem(me + 1 + d // q, 2)
 
     def fetch(c, d):
         at = (c * n + peer(d)) * k
@@ -107,12 +111,18 @@
             device_id=(z, peer(d)), device_id_type=MESH,
         )
 
-    def block_copy(c, d):
-        j = peer(d)
-        return pltpu.make_async_remote_copy(
-            src_ref=send.at[c, j], dst_ref=recv.at[c, me],
+    def sibling_copy(c):
+        return pltpu.make_async_remote_copy(
+            src_ref=sib_send.at[c], dst_ref=sib_recv.at[c],
+            send_sem=sib_ssem.at[c], recv_sem=sib_rsem.at[c],
+            device_id=(z, sibling), device_id_type=MESH,
+        )
+
+    def block_copy(c, chip):
+        return pltpu.make_async_remote_copy(
+            src_ref=mine.at[c, chip], dst_ref=recv.at[c, my_chip],
             send_sem=send_sem.at[c], recv_sem=recv_sem.at[c],
-            device_id=(z, j), device_id_type=MESH,
+            device_id=(z, chip * 2 + core), device_id_type=MESH,
         )
 
     span = soc_v.shape[-1]
@@ -146,24 +156,33 @@
     same = iota((lanes, lanes), 0) // width == iota((lanes, lanes), 1) // width
     fold_w[...] = jnp.where(same, -1.5 * wide, 0.0)
 
+    def half(c, first, target):
+        for g in range(q // group):
+            at = first + g * group
+            for i, block in enumerate(transform(c, at)):
+                target[c, lax.rem(my_chip + 1 + g * group + i, q)] = block
+
+    def forward(c):
+        sibling_copy(c).wait_recv()
+        for i in range(q - 1):
+            chip = lax.rem(my_chip + 1 + i, q)
+            mine[c, chip] = mine[c, chip] + sib_recv[c, chip]
+            block_copy(c, chip).start()
+        recv[c, my_chip] = mine[c, my_chip] + sib_recv[c, my_chip]
+
+    half(0, 0, sib_send)
+    sibling_copy(0).start()
+    half(0, q, mine)
+
     def chunk(c, carry):
-        def one(g, carry):
-            for i, block in enumerate(transform(c, g * group)):
-                send[c, peer(g * group + i)] = block
-                block_copy(c, g * group + i).start()
-            return carry
-
-        lax.fori_loop(0, n // group - 1, one, 0)
-        last = n - group
-        for i, block in enumerate(transform(c, last)):
-            if i < group - 1:
-                send[c, peer(last + i)] = block
-                block_copy(c, last + i).start()
-            else:
-                recv[c, me] = block
+        half(c, 0, sib_send)
+        sibling_copy(c).start()
+        forward(c - 1)
+        half(c, q, mine)
         return carry
 
-    lax.fori_loop(0, chunks, chunk, 0)
+    lax.fori_loop(1, chunks, chunk, 0)
+    forward(chunks - 1)
 
     pltpu.make_async_copy(
         dens_all.at[pl.ds(0, n - 1)], dens_all.at[pl.ds(0, n - 1)], drecv_sem
@@ -187,10 +206,10 @@
 
     total = []
     for c in range(chunks):
-        block = recv.at[c, pl.ds(0, n - 1)]
+        block = recv.at[c, pl.ds(0, q - 1)]
         pltpu.make_async_copy(block, block, recv_sem.at[c]).wait()
         summed = recv[c, 0]
-        for s in range(1, n):
+        for s in range(1, q):
             summed = summed + recv[c, s]
         total.append(summed)
 
@@ -262,7 +281,8 @@
         dens_all.at[pl.ds(0, n - 1)], dens_all.at[pl.ds(0, n - 1)], dsend_sem
     ).wait()
     for c in range(chunks):
-        block = send.at[c, pl.ds(0, n - 1)]
+        sibling_copy(c).wait_send()
+        block = mine.at[c, pl.ds(0, q - 1)]
         pltpu.make_async_copy(block, block, send_sem.at[c]).wait()
     block = part_a.at[pl.ds(0, n - 1)]
     pltpu.make_async_copy(block, block, asend_sem).wait()
@@ -296,8 +316,10 @@
             dma((6,)),
             pltpu.VMEM((slab, parts * width, span), jnp.bfloat16),
             pltpu.VMEM((slab, width, span), jnp.bfloat16),
-            pltpu.VMEM((chunks, n, width, block), jnp.float32),
-            pltpu.VMEM((chunks, n, width, block), jnp.float32),
+            pltpu.VMEM((chunks, n // 2, width, block), jnp.float32),
+            pltpu.VMEM((chunks, n // 2, width, block), jnp.float32),
+            pltpu.VMEM((chunks, n // 2, width, block), jnp.float32),
+            pltpu.VMEM((chunks, n // 2, width, block), jnp.float32),
             pltpu.VMEM((16, cells), jnp.bfloat16),
             pltpu.VMEM((n, 16, cells), jnp.bfloat16),
             pltpu.VMEM((rows_p, cells), jnp.float32),
@@ -305,7 +327,7 @@
             pltpu.VMEM((width * k, width * k), jnp.float32),
             pltpu.VMEM((n, 8, rows_p), jnp.float32),
             pltpu.VMEM((m, 8, rows_p), jnp.float32),
-            dma((chunks, n)), dma((chunks, n)), dma((chunks,)), dma((chunks,)),
+            dma((chunks, n)), dma((chunks, n)), dma((chunks,)), dma((chunks,)), dma((chunks,)), dma((chunks,)),
             dma, dma, dma, dma, dma, dma,
         ],
         compiler_params=pltpu.CompilerParams(

time: 25.1 us -> 25.6 us (1.020)
  Pallas kernels: 23.6 us -> 24.1 us
    pallas_call x1, Pallas kernels: 23.6 us -> 24.1 us  [on_device(): pl.pallas_call(functools.partial(kernel, n, m, chunks, k, 4, scale), out_...]
where the time goes in v4:
time: 25.6 us; the launch traced here: 25.4 us
  Pallas kernels  24.1 us (94%)
  local copies, waits for them, and re-layouts  1.26 us (5%)
    pallas_call x1, Pallas kernels, on_device(): pl.pallas_call(functools.partial(kernel, n, m, chunks, k, 4, scale), out_...  24.1 us
    unnamed x1, local copies, waits for them, and re-layouts  1.26 us

profile of v4, /device:TPU:0, one launch (start us, length us, event | category | flops | bytes accessed | tf_op | source)
XLA Modules:
  0.0 25.4 jit_solution(10939689791001059858)
XLA Ops:
  0.0 24.1 %shard_map.82 = f32[3,10]{1,0:T(4,128)} custom-call(bf16[128,48,1024]{2,1,0:T(8,128)(2,1)} %bitcast.4, bf16[128,16,1024]{2,1,0:T(8,128)(2,1)} %cou_ref.1, bf16[16,1024]{1,0:T(8,128)(2,1)} %coef_hbm.1, f32[16,16]{1,0:T(8,128)} %rdm_hbm.1, bf16[10,256]{1,0:T(8,128)(2,1)} %dens_hbm.1, s32[2,80]{1,0:T(2,128)} %bitcast.5, s32[1,10]{1,0:T(1,128)} %bitcast.6, ...), custom_call_target="tpu_custom_call" | custom-call | flops 268435456 | bytes 16777216 | tf_op jit(solution)/shard_map/pallas_call | solution.py:304
  24.2 1.3 %copy.10 = f32[3,10]{1,0:T(4,128)} copy(f32[3,10]{1,0:T(4,128)} %shard_map.82) | data formatting | bytes 240

commit v5 on v2

--- a/solution.py
+++ b/solution.py
@@ -58,19 +58,15 @@
         chip = lax.rem(me // 2 + 1 + d // 2, n // 2)
         return chip * 2 + lax.rem(me + 1 + d, 2)
 
-    def fetch(c, d):
-        at = (c * n + peer(d)) * k
+    def fetch(c):
+        part = pl.ds(c * n * k, n * k)
         return (
-            pltpu.make_async_copy(soc_ref.at[pl.ds(at, k)], soc_v.at[pl.ds(at, k)], soc_sem.at[c, d]),
-            pltpu.make_async_copy(cou_ref.at[pl.ds(at, k)], cou_v.at[pl.ds(at, k)], cou_sem.at[c, d]),
-        )
-
-    def start_fetch(i, carry):
-        for copy in fetch(i // n, lax.rem(i, n)):
-            copy.start()
-        return carry
-
-    lax.fori_loop(0, group, start_fetch, 0)
+            pltpu.make_async_copy(soc_ref.at[part], soc_v.at[part], soc_sem.at[c]),
+            pltpu.make_async_copy(cou_ref.at[part], cou_v.at[part], cou_sem.at[c]),
+        )
+
+    for copy in fetch(0):
+        copy.start()
     small = [
         pltpu.make_async_copy(a, b, small_sem.at[i])
         for i, (a, b) in enumerate([
@@ -89,7 +85,9 @@
             barrier, inc=1, device_id=(lax.rem(z + 1 + d, m), me), device_id_type=MESH
         )
 
-    lax.fori_loop(group, chunks * n, start_fetch, 0)
+    for c in range(1, chunks):
+        for copy in fetch(c):
+            copy.start()
     for copy in small:
         copy.wait()
 
@@ -119,9 +117,6 @@
     block_rows = 4 * width * k
 
     def transform(c, first):
-        for i in range(group):
-            for copy in fetch(c, first + i):
-                copy.wait()
         rows = []
         for i in range(group):
             at = (c * n + peer(first + i)) * k
@@ -147,6 +142,9 @@
     fold_w[...] = jnp.where(same, -1.5 * wide, 0.0)
 
     def chunk(c, carry):
+        for copy in fetch(c):
+            copy.wait()
+
         def one(g, carry):
             for i, block in enumerate(transform(c, g * group)):
                 send[c, peer(g * group + i)] = block
@@ -305,7 +303,7 @@
             pltpu.VMEM((width * k, width * k), jnp.float32),
             pltpu.VMEM((n, 8, rows_p), jnp.float32),
             pltpu.VMEM((m, 8, rows_p), jnp.float32),
-            dma((chunks, n)), dma((chunks, n)), dma((chunks,)), dma((chunks,)),
+            dma((chunks,)), dma((chunks,)), dma((chunks,)), dma((chunks,)),
             dma, dma, dma, dma, dma, dma,
         ],
         compiler_params=pltpu.CompilerParams(

time: 25.1 us -> 24.5 us (0.976)
  Pallas kernels: 23.6 us -> 23.1 us
    pallas_call x1, Pallas kernels: 23.6 us -> 23.1 us  [on_device(): pl.pallas_call(functools.partial(kernel, n, m, chunks, k, 4, scale), out_...]
where the time goes in v5:
time: 24.5 us; the launch traced here: 24.4 us
  Pallas kernels  23.1 us (94%)
  local copies, waits for them, and re-layouts  1.26 us (5%)
    pallas_call x1, Pallas kernels, on_device(): pl.pallas_call(functools.partial(kernel, n, m, chunks, k, 4, scale), out_...  23.1 us
    unnamed x1, local copies, waits for them, and re-layouts  1.26 us

profile of v5, /device:TPU:0, one launch (start us, length us, event | category | flops | bytes accessed | tf_op | source)
XLA Modules:
  0.0 24.4 jit_solution(1186426823687066932)
XLA Ops:
  0.0 23.1 %shard_map.82 = f32[3,10]{1,0:T(4,128)} custom-call(bf16[128,48,1024]{2,1,0:T(8,128)(2,1)} %bitcast.4, bf16[128,16,1024]{2,1,0:T(8,128)(2,1)} %cou_ref.1, bf16[16,1024]{1,0:T(8,128)(2,1)} %coef_hbm.1, f32[16,16]{1,0:T(8,128)} %rdm_hbm.1, bf16[10,256]{1,0:T(8,128)(2,1)} %dens_hbm.1, s32[2,80]{1,0:T(2,128)} %bitcast.5, s32[1,10]{1,0:T(1,128)} %bitcast.6, ...), custom_call_target="tpu_custom_call" | custom-call | flops 268435456 | bytes 16777216 | tf_op jit(solution)/shard_map/pallas_call | solution.py:282
  23.1 1.3 %copy.10 = f32[3,10]{1,0:T(4,128)} copy(f32[3,10]{1,0:T(4,128)} %shard_map.82) | data formatting | bytes 240
